TPU v7x, 32 devices: a whole 2x2x4 slice. The times are simulated.
32 devices in a mesh: groups: 2 (over x), tm: 16 (over z, y, core).
Axes of the slice: x: 2, y: 2, z: 4, core: 2. Of those that a mesh axis runs over, the one named last changes fastest.
Arguments:
- trans_matrix: bfloat16 [1024, 1024], replicated, may hold values from -1 to 1
- ensemble: bfloat16 [1024, 128], replicated, may hold values from -16 to 16
- obs_operator: bfloat16 [32, 256, 256], P(('groups', 'tm')), parts along dimension 0, may hold values from -0.375 to 0.375
- pattern: int32 [32, 2, 2], P(('groups', 'tm')), parts along dimension 0, may hold values from 0 to 7, as said below
- counts: int32 [32], P(('groups', 'tm')), parts along dimension 0, may hold values from 64 to 256, as said below
- observations: float32 [32, 256], P(('groups', 'tm')), parts along dimension 0, may hold values from -6 to 6
- obs_variance: float32 [32, 256], P(('groups', 'tm')), parts along dimension 0, may hold values from 0.04 to 8
- initial_state: float32 [2048], P('groups'), parts along dimension 0, may hold values from -6 to 6
Outputs:
- states: float32 [32, 1024], P(('groups', 'tm')), parts along dimension 0
- misfit: float32 [2], P('groups'), parts along dimension 0
There are 2 independent parts, one for each index of `groups`. A program takes and returns all parts, laid end to end along the dimension named above; an argument that names none is the same for every part. Nothing has to cross between parts.
Inputs may be any that keep to these rules, and one draw needn't show every extreme that they name: `pattern`: the 2 entries of a row name different blocks. `counts`: some step has all 256 rows live.
All inputs are finite; a program needn't handle non-finite values.
Results may differ from a plain program's by a relative error of at most 0.02.
Values may be sent and summed in bfloat16 or wider, within the bound.
A program may use at most 512 MiB of HBM per device.

v0:
```python
import jax
import jax.numpy as jnp
from jax import lax
from jax.sharding import PartitionSpec as P

N = 1024
BLK = 128
NB = 8
MB = 2
KB = 2
MOBS = 256
NE = 128


def entering(part, axis, combine, identity):
    place = lax.axis_index(axis)
    gathered = jax.tree.map(lambda a: lax.all_gather(a, axis), part)
    state = jax.tree.map(lambda a, e: jnp.zeros_like(a) + jnp.asarray(e, a.dtype), part, identity)

    def one(step, state):
        return combine(
            state, jax.tree.map(lambda a: lax.dynamic_index_in_dim(a, step, 0, False), gathered)
        )

    return lax.fori_loop(0, place, one, state)


def split_three(vector):
    high = vector.astype(jnp.bfloat16)
    rest = vector - high.astype(jnp.float32)
    middle = rest.astype(jnp.bfloat16)
    lowest = (rest - middle.astype(jnp.float32)).astype(jnp.bfloat16)
    return jnp.stack([high, middle, lowest], axis=0)


def join_three(stacked):
    wide = stacked.astype(jnp.float32)
    return wide[0] + wide[1] + wide[2]


def apply_matrix(matrix, vector):
    stacked = split_three(vector)
    parts = jnp.einsum("ij,kj->ki", matrix, stacked, preferred_element_type=jnp.float32)
    return parts[0] + parts[1] + parts[2]


def element_maps(trans_matrix, ensemble, hrows, cols, count, yobs, rvar):
    fcols = trans_matrix.reshape(NB, BLK, N)[cols].reshape(MB, KB * BLK, N)
    ecols = ensemble.reshape(NB, BLK, NE)[cols].reshape(MB, KB * BLK, NE)
    hblock = hrows.reshape(MB, BLK, KB * BLK)
    active_rows = (lax.iota(jnp.int32, MOBS) < count).astype(jnp.float32)
    forward = (
        jnp.einsum("mrk,mkn->mrn", hblock, fcols, preferred_element_type=jnp.float32).reshape(
            MOBS, N
        )
        * active_rows[:, None]
    )
    member = (
        jnp.einsum("mrk,mkn->mrn", hblock, ecols, preferred_element_type=jnp.float32).reshape(
            MOBS, NE
        )
        * active_rows[:, None]
    )
    covariance = jnp.dot(member, member.T, precision=lax.Precision.HIGHEST) / NE + jnp.diag(rvar)
    factor = jnp.linalg.cholesky(covariance)
    solved = jax.scipy.linalg.cho_solve((factor, True), member)
    masked_obs = yobs * active_rows
    reduced = (jnp.dot(solved.T, forward, precision=lax.Precision.HIGHEST) / NE).astype(
        jnp.bfloat16
    )
    transit = (
        trans_matrix.astype(jnp.float32)
        - jnp.dot(ensemble, reduced, preferred_element_type=jnp.float32)
    ).astype(jnp.bfloat16)
    weights = jnp.dot(solved.T, masked_obs, precision=lax.Precision.HIGHEST) / NE
    offset = jnp.dot(ensemble.astype(jnp.float32), weights, precision=lax.Precision.HIGHEST)
    return (transit, offset, forward, factor, masked_obs)


def compose(earlier, latter):
    product = jnp.dot(latter[0], earlier[0], preferred_element_type=jnp.float32).astype(
        jnp.bfloat16
    )
    vector = apply_matrix(latter[0], join_three(earlier[1])) + join_three(latter[1])
    return (product, split_three(vector))


def shards(
    trans_matrix, ensemble, obs_operator, pattern, counts, observations, obs_variance, initial_state
):
    transit, offset, forward, factor, masked_obs = element_maps(
        trans_matrix,
        ensemble,
        obs_operator[0],
        pattern[0],
        counts[0],
        observations[0],
        obs_variance[0],
    )
    identity = (jnp.eye(N, dtype=jnp.bfloat16), jnp.zeros((3, N), jnp.bfloat16))
    prefix = entering((transit, split_three(offset)), "tm", compose, identity)
    incoming = apply_matrix(prefix[0], initial_state) + join_three(prefix[1])
    current = apply_matrix(transit, incoming) + offset
    innovation = masked_obs - jnp.dot(forward, incoming, precision=lax.Precision.HIGHEST)
    quadratic = jnp.sum(innovation * jax.scipy.linalg.cho_solve((factor, True), innovation))
    totals = lax.psum((quadratic, counts[0].astype(jnp.float32)), "tm")
    misfit = (totals[0] / totals[1]).reshape(1)
    return (current.reshape(1, N), misfit)


def solution(mesh):
    return jax.shard_map(
        shards,
        mesh=mesh,
        in_specs=(
            P(),
            P(),
            P(("groups", "tm"), None, None),
            P(("groups", "tm"), None, None),
            P(("groups", "tm")),
            P(("groups", "tm"), None),
            P(("groups", "tm"), None),
            P("groups"),
        ),
        out_specs=(P(("groups", "tm"), None), P("groups")),
        check_vma=False,
    )
```

profile of v0, /device:TPU:0, one launch (start us, length us, event | category | flops | bytes accessed | tf_op | source)
XLA Modules:
  0.0 444.8 jit_solution(17466215086710972942)
XLA Ops:
  7.2 0.0 copy-start
  7.2 0.0 all-gather.5.cloned.1.call-start
  7.9 0.7 compare_select_fusion
  8.6 0.1 reshape.179
  8.7 0.6 gather_fusion
  9.3 1.1 bitcast_multiply_fusion.3
  10.4 0.4 convolution_multiply_fusion.1
  10.8 0.1 copy.14
  10.9 0.9 add_multiply_fusion
  11.8 11.7 %cholesky.49 = f32[128,128]{1,0:T(8,128)S(1)} custom-call(f32[128,128]{1,0:T(8,128)S(1)} %cholesky.115), custom_call_target="Cholesky" | custom-call | tf_op jit(solution)/shard_map/jit(cholesky)/cholesky | solution.py:65
  23.5 9.8 %custom-call.24 = f32[1,128,128]{1,2,0:T(8,128)S(1)} custom-call(f32[1,128,128]{2,1,0:T(8,128)S(1)} %get-tuple-element.95), custom_call_target="InvertDiagBlocksLowerTriangular" | custom-call | tf_op jit(solution)/shard_map/jit(cholesky)/cholesky | solution.py:65
  33.4 0.2 constant_dynamic-update-slice_fusion.1
  33.6 0.3 convolution_subtract_fusion.2
  33.9 11.7 %cholesky.103 = f32[128,128]{1,0:T(8,128)S(1)} custom-call(f32[128,128]{1,0:T(8,128)S(1)} %convolution_subtract_fusion.2), custom_call_target="Cholesky" | custom-call | tf_op jit(solution)/shard_map/jit(cholesky)/cholesky | solution.py:65
  45.6 0.7 compare_reduce_fusion
  47.5 0.1 triangular_solve.100
  47.6 3.9 while.14
  47.7 0.6 fusion.128
  48.3 1.3 bitcast_dynamic-update-slice_fusion.2
  49.6 0.6 fusion.128
  50.2 1.3 bitcast_dynamic-update-slice_fusion.2
  51.5 19.7 %custom-call.25 = f32[2,128,128]{1,2,0:T(8,128)S(1)} custom-call(f32[2,128,128]{2,1,0:T(8,128)S(1)} %get-tuple-element.45), custom_call_target="InvertDiagBlocksLowerTriangular" | custom-call | tf_op jit(solution)/shard_map/jit(_cho_solve)/triangular_solve | solution.py:66
  71.2 0.1 bitcast_multiply_fusion.2
  71.3 0.3 fusion.31
  71.6 0.2 convolution_subtract_fusion.1
  71.8 0.3 fusion.39
  72.1 0.2 fusion.38
  72.3 0.3 convolution_subtract_fusion
  72.6 0.8 fusion.37
  73.5 2.9 copy.13
  76.4 3.2 gather_fusion.1
  79.5 1.6 bitcast_multiply_fusion.1
  81.2 0.1 bitcast_multiply_fusion
  81.3 0.0 copy-done.6
  81.3 0.0 copy-done.8
  81.3 0.7 fusion.23
  82.1 2.1 fusion.21
  84.2 0.0 all-gather.5.cloned.1.call-update
  84.2 0.6 copy-done.10
  84.9 0.2 copy-done.7
  85.0 0.0 copy-done.9
  85.1 0.2 fusion.29
  85.2 0.3 fusion.78
  85.6 0.0 copy-done.12
  85.7 23.9 %all-gather.2 = bf16[16,3,1024]{2,1,0:T(4,128)(2,1)S(1)} all-gather(bf16[1,3,1024]{2,1,0:T(4,128)(2,1)S(1)} %maximum_bitcast_fusion), channel_id=3, replica_groups=mesh['groups'=2,'tm'=16] {'tm'}, dimensions={0}, use_global_device_ids=true | all-gather | bytes 104448 | tf_op jit(solution)/shard_map/all_gather | solution.py:17
  109.6 0.3 fusion.22
  109.9 145.7 %all-gather.5.cloned.1.call-done = bf16[16384,1024]{0,1:T(8,128)(2,1)} async-done(((bf16[1024,1024]{0,1:T(8,128)(2,1)}), bf16[16384,1024]{0,1:T(8,128)(2,1)}) %all-gather.5.cloned.1.call-update) | async-done | bytes 33554448 | tf_op jit(solution)/shard_map/all_gather | solution.py:17
  255.6 44.0 %copy.16 = bf16[16384,1024]{1,0:T(8,128)(2,1)} copy(bf16[16384,1024]{0,1:T(8,128)(2,1)} %all-gather.5.cloned.1.call-done) | data formatting | bytes 67108864 | tf_op jit(solution)/shard_map/while | solution.py:25
  299.7 0.0 copy-start.1
  299.7 0.6 fusion.44
  300.4 0.9 fusion.57
  301.3 0.0 copy-done.11
  301.4 0.2 fusion.36
  301.5 0.0 copy-done.4
  301.5 0.2 fusion.27
  301.7 0.2 convolution_bitcast_fusion.3
  301.9 0.2 convolution_bitcast_fusion.2
  302.1 0.2 fusion.25
  302.3 0.2 convolution_bitcast_fusion
  302.5 0.7 multiply_reduce_fusion
  303.2 0.0 copy-done.2
  303.2 0.4 fusion.50
  303.6 0.6 add.171
  304.2 131.3 %all-reduce.1 = (f32[]{:T(128)}, f32[]{:T(128)}) all-reduce(f32[]{:T(128)} %multiply_reduce_fusion, f32[]{:T(128)S(6)} %convert_element_type.163), channel_id=1, replica_groups=mesh['groups'=2,'tm'=16] {'tm'}, use_global_device_ids=true, to_apply=%region_7.8 | all-reduce | flops 2 | bytes 16 | tf_op jit(solution)/shard_map/psum | solution.py:106
  (46 shorter events, 0.4 us)
Async XLA Ops:
  7.2 1.6 copy-start
  7.2 248.4 %all-gather.5.cloned.1.call-start = ((), (), s32[]{:S(2)}) async-start(), calls=%async_computation | async-start | bytes 35651584 | tf_op jit(solution)/shard_map/all_gather | solution.py:17
  51.5 24.8 %copy-start.3 = (f32[256,256]{1,0:T(8,128)}, f32[256,256]{1,0:T(8,128)S(1)}, u32[]{:S(2)}) copy-start(f32[256,256]{1,0:T(8,128)S(1)} %get-tuple-element.240) | copy-start | bytes 786436
  72.3 4.0 copy-start.5
  79.5 1.8 copy-start.6
  79.5 1.8 copy-start.8
  84.2 0.7 copy-start.10
  84.2 0.9 copy-start.7
  84.2 0.9 copy-start.9
  84.2 1.4 copy-start.12
  299.7 1.7 copy-start.11
  299.7 1.8 copy-start.4
  299.7 3.5 copy-start.2
  299.7 137.1 %copy-start.1 = (bf16[1024,128]{1,0:T(8,128)(2,1)S(1)}, bf16[1024,128]{1,0:T(8,128)(2,1)}, u32[]{:S(2)}) copy-start(bf16[1024,128]{1,0:T(8,128)(2,1)} %param.11) | copy-start | bytes 786436
Sparse Core Ops, SparseCore 0:
  84.3 171.2 all-gather.4
where the time goes:
time: 447 us; the launch traced here: 445 us
  blocking collectives  155 us (35%)
  waiting for transfers between devices  146 us (33%)
  other arithmetic  57.1 us (13%)
  local copies, waits for them, and re-layouts  55.7 us (12%)
  between operations  18.8 us (4%)
  matrix products  12 us (3%)
    all_gather x1, waiting for transfers between devices, entering(): gathered = jax.tree.map(lambda a: lax.all_gather(a, axis), part)  146 us
    psum x1, blocking collectives, shards(): totals = lax.psum((quadratic, counts[0].astype(jnp.float32)), 'tm')  131 us
    while x1, local copies, waits for them, and re-layouts, entering(): return lax.fori_loop(0, place, one, state)  44 us
    another operation x6, other arithmetic, element_maps(): factor = jnp.linalg.cholesky(covariance)  34 us
    all_gather x1, blocking collectives, entering(): gathered = jax.tree.map(lambda a: lax.all_gather(a, axis), part)  23.9 us
    another operation x3, other arithmetic, element_maps(): solved = jax.scipy.linalg.cho_solve((factor, True), member)  19.7 us
  transfers between devices with their start and end apart: 1, of which 1 were waited for; matrix products, arithmetic and copies ran while one was open for 0% of the time, Pallas kernels for 0%

commit v1 on v0

v1 whole, which is shorter than its diff:
```python
import functools

import jax
import jax.numpy as jnp
from jax import lax
from jax.experimental import pallas as pl
from jax.experimental.pallas import tpu as pltpu
from jax.sharding import PartitionSpec as P

N = 1024
BLK = 128
NB = 8
MB = 2
KB = 2
MOBS = 256
NE = 128
HIGH = lax.Precision.HIGHEST
VMEM = pl.BlockSpec(memory_space=pltpu.VMEM)
SMEM = pl.BlockSpec(memory_space=pltpu.SMEM)


def times(left, right, precision=None):
    return lax.dot_general(
        left, right, (((1,), (0,)), ((), ())), precision=precision, preferred_element_type=jnp.float32
    )


def times_t(left, right, precision=None):
    return lax.dot_general(
        left, right, (((1,), (1,)), ((), ())), precision=precision, preferred_element_type=jnp.float32
    )


def maps_kernel(
    pattern, count, trans, ensemble, hrows, yobs, rvar,
    transit, offset, forward, gain, member, dinv, masked, swept,
):
    live = count[0]
    rows = lax.broadcasted_iota(jnp.int32, (MOBS, 1), 0)
    active_rows = (rows < live).astype(jnp.float32)
    lanes = lax.broadcasted_iota(jnp.int32, (1, MOBS), 1)
    active_lanes = (lanes < live).astype(jnp.float32)
    for m in range(MB):
        here = pl.ds(m * BLK, BLK)
        starts = [pl.multiple_of(pattern[0, m, k] * BLK, BLK) for k in range(KB)]
        hblock = hrows[0, here, :]
        ecols = jnp.concatenate([ensemble[pl.ds(s, BLK), :] for s in starts], axis=0)
        fcols = jnp.concatenate([trans[pl.ds(s, BLK), :] for s in starts], axis=0)
        alive = active_rows[m * BLK : (m + 1) * BLK]
        member[here, :] = times(hblock, ecols) * alive
        forward[here, :] = times(hblock, fcols) * alive
    inverse_var = active_lanes / rvar[...]
    dinv[...] = inverse_var
    masked[...] = yobs[...] * active_lanes
    scaled = member[...].T * inverse_var
    row = lax.broadcasted_iota(jnp.int32, (NE, NE), 0)
    lane = lax.broadcasted_iota(jnp.int32, (NE, NE), 1)
    start = times(scaled, member[...], HIGH) / NE + (row == lane).astype(jnp.float32)
    swept[...] = (start + start.T) * 0.5

    def sweep(k, carry):
        x = swept[...]
        r = swept[pl.ds(k, 1), :]
        on_lane = lane == k
        on_row = row == k
        c = jnp.sum(jnp.where(on_lane, x, 0.0), axis=1, keepdims=True)
        one_lane = lax.broadcasted_iota(jnp.int32, (1, NE), 1) == k
        pivot = jnp.sum(jnp.where(one_lane, r, 0.0), axis=1, keepdims=True)
        inv = 1.0 / pivot
        scaled_r = jnp.where(one_lane, -inv, r * inv)
        out = jnp.where(on_lane, c * inv, x - c * scaled_r)
        swept[...] = jnp.where(on_row, scaled_r, out)
        return carry

    lax.fori_loop(0, NE, sweep, 0)
    gains = times(-swept[...], scaled, HIGH) / NE
    gain[...] = gains
    reduced = times(gains, forward[...], HIGH).astype(jnp.bfloat16)
    transit[...] = (trans[...].astype(jnp.float32) - times(ensemble[...], reduced)).astype(
        jnp.bfloat16
    )
    seen = jnp.broadcast_to(masked[...], (8, MOBS))
    weights = times_t(seen, gains, HIGH)
    offset[...] = times_t(weights, ensemble[...].astype(jnp.float32), HIGH)[:1]


def split_rows(vector):
    high = vector.astype(jnp.bfloat16).astype(jnp.float32)
    rest = vector - high
    middle = rest.astype(jnp.bfloat16).astype(jnp.float32)
    lowest = rest - middle
    row = lax.broadcasted_iota(jnp.int32, (16, N), 0)
    stacked = jnp.where(row == 0, high, jnp.where(row == 1, middle, jnp.where(row == 2, lowest, 0.0)))
    return stacked.astype(jnp.bfloat16)


def chain_kernel(
    n, count, transit, offset, forward, gain, member, dinv, masked, first,
    states, misfit,
    incoming, current, produced, tiles, send_sem, recv_sem, tile_send, tile_recv,
):
    me = lax.axis_index("tm")
    barrier = pltpu.get_barrier_semaphore()

    def greet(i, carry):
        pl.semaphore_signal(barrier, inc=1, device_id={"tm": lax.rem(me + i, n)})
        return carry

    lax.fori_loop(1, n, greet, 0)
    pl.semaphore_wait(barrier, n - 1)

    pass_on = pltpu.make_async_remote_copy(
        src_ref=produced,
        dst_ref=incoming,
        send_sem=send_sem,
        recv_sem=recv_sem,
        device_id={"tm": lax.rem(me + 1, n)},
    )

    @pl.when(me == 0)
    def _():
        current[...] = first[...]

    @pl.when(me > 0)
    def _():
        pass_on.wait_recv()
        current[...] = incoming[...]

    before = current[...]
    parts = times_t(split_rows(before), transit[...])
    after = jnp.sum(parts, axis=0, keepdims=True) + offset[...]
    produced[...] = after

    @pl.when(me < n - 1)
    def _():
        pass_on.start()

    states[...] = after
    innovation = jnp.broadcast_to(masked[...], (8, MOBS)) - times_t(
        jnp.broadcast_to(before, (8, N)), forward[...], HIGH
    )
    moved = times_t(innovation, gain[...], HIGH)
    left = innovation - times_t(moved, member[...], HIGH)
    fit = jnp.sum(left * left * dinv[...], axis=1, keepdims=True) + NE * jnp.sum(
        moved * moved, axis=1, keepdims=True
    )
    lane = lax.broadcasted_iota(jnp.int32, (8, NE), 1)
    live = count[0].astype(jnp.float32)
    tiles[me] = jnp.where(lane == 0, fit, live)

    def tell(i):
        return pltpu.make_async_remote_copy(
            src_ref=tiles.at[me],
            dst_ref=tiles.at[me],
            send_sem=tile_send.at[i],
            recv_sem=tile_recv.at[me],
            device_id={"tm": lax.rem(me + i, n)},
        )

    def hear(i):
        other = lax.rem(me + n - i, n)
        return pltpu.make_async_remote_copy(
            src_ref=tiles.at[other],
            dst_ref=tiles.at[other],
            send_sem=tile_send.at[i],
            recv_sem=tile_recv.at[other],
            device_id={"tm": other},
        )

    def start(i, carry):
        tell(i).start()
        return carry

    def finish(i, carry):
        hear(i).wait_recv()
        return carry

    def sent(i, carry):
        tell(i).wait_send()
        return carry

    lax.fori_loop(1, n, start, 0)
    lax.fori_loop(1, n, finish, 0)
    lax.fori_loop(1, n, sent, 0)

    @pl.when(me < n - 1)
    def _():
        pass_on.wait_send()

    total = jnp.sum(tiles[...], axis=0)[:1]
    one = lax.broadcasted_iota(jnp.int32, (1, NE), 1)
    fits = jnp.sum(jnp.where(one == 0, total, 0.0), axis=1, keepdims=True)
    lives = jnp.sum(jnp.where(one == 1, total, 0.0), axis=1, keepdims=True)
    misfit[...] = jnp.broadcast_to(fits / lives, (1, NE))


def shards(
    n, trans_matrix, ensemble, obs_operator, pattern, counts, observations, obs_variance, initial_state
):
    f32 = jnp.float32
    transit, offset, forward, gain, member, dinv, masked = pl.pallas_call(
        maps_kernel,
        out_shape=(
            jax.ShapeDtypeStruct((N, N), jnp.bfloat16),
            jax.ShapeDtypeStruct((1, N), f32),
            jax.ShapeDtypeStruct((MOBS, N), f32),
            jax.ShapeDtypeStruct((NE, MOBS), f32),
            jax.ShapeDtypeStruct((MOBS, NE), f32),
            jax.ShapeDtypeStruct((1, MOBS), f32),
            jax.ShapeDtypeStruct((1, MOBS), f32),
        ),
        in_specs=[SMEM, SMEM] + [VMEM] * 5,
        out_specs=(VMEM,) * 7,
        scratch_shapes=[pltpu.VMEM((NE, NE), f32)],
        compiler_params=pltpu.CompilerParams(vmem_limit_bytes=48 * 1024 * 1024),
        name="maps",
    )(pattern, counts, trans_matrix, ensemble, obs_operator, observations, obs_variance)
    states, misfit = pl.pallas_call(
        functools.partial(chain_kernel, n),
        out_shape=(jax.ShapeDtypeStruct((1, N), f32), jax.ShapeDtypeStruct((1, NE), f32)),
        in_specs=[SMEM] + [VMEM] * 8,
        out_specs=(VMEM, VMEM),
        scratch_shapes=[
            pltpu.VMEM((1, N), f32),
            pltpu.VMEM((1, N), f32),
            pltpu.VMEM((1, N), f32),
            pltpu.VMEM((n, 8, NE), f32),
            pltpu.SemaphoreType.DMA,
            pltpu.SemaphoreType.DMA,
            pltpu.SemaphoreType.DMA((n,)),
            pltpu.SemaphoreType.DMA((n,)),
        ],
        compiler_params=pltpu.CompilerParams(
            collective_id=0, has_side_effects=True, vmem_limit_bytes=48 * 1024 * 1024
        ),
        name="chain",
    )(counts, transit, offset, forward, gain, member, dinv, masked, initial_state.reshape(1, N))
    return states, misfit[0, :1]


def solution(mesh):
    return jax.shard_map(
        functools.partial(shards, mesh.shape["tm"]),
        mesh=mesh,
        in_specs=(
            P(),
            P(),
            P(("groups", "tm"), None, None),
            P(("groups", "tm"), None, None),
            P(("groups", "tm")),
            P(("groups", "tm"), None),
            P(("groups", "tm"), None),
            P("groups"),
        ),
        out_specs=(P(("groups", "tm"), None), P("groups")),
        check_vma=False,
    )
```

time: 447 us -> 80.9 us (0.18)
  blocking collectives: 155 us -> 0 us
  waiting for transfers between devices: 146 us -> 0 us
  Pallas kernels: 0 us -> 72.1 us
  other arithmetic: 57.1 us -> 0 us
  local copies, waits for them, and re-layouts: 55.7 us -> 6.07 us
  between operations: 18.8 us -> 2.47 us
  matrix products: 12 us -> 0 us
    all_gather x1 -> x0, waiting for transfers between devices: 146 us -> none  [entering(): gathered = jax.tree.map(lambda a: lax.all_gather(a, axis), part)]
    psum x1 -> x0, blocking collectives: 131 us -> none  [shards(): totals = lax.psum((quadratic, counts[0].astype(jnp.float32)), 'tm')]
    pallas_call x0 -> x2, Pallas kernels: none -> 72.1 us  [the longest x1 55.6 us: shards(): pl.pallas_call(functools.partial(chain_kernel, n), out_shape=(jax.ShapeDt...]
    another operation x10 -> x0, other arithmetic: 53.7 us -> none  [the longest x6 34 us: element_maps(): factor = jnp.linalg.cholesky(covariance)]
    while x1 -> x0, local copies, waits for them, and re-layouts: 44 us -> none  [entering(): return lax.fori_loop(0, place, one, state)]
    all_gather x1 -> x0, blocking collectives: 23.9 us -> none  [entering(): gathered = jax.tree.map(lambda a: lax.all_gather(a, axis), part)]
    dot_general x10 -> x0, matrix products: 8.34 us -> none  [the longest x1 2.1 us: element_maps(): jnp.dot(ensemble, reduced, preferred_element_type=jnp.float32)]
  transfers between devices with their start and end apart: 1 -> 0, of which waited for: 1 -> 0; matrix products, arithmetic and copies ran while one was open for 0% -> 0% of each run, Pallas kernels for 0% -> 0%
where the time goes in v1:
time: 80.9 us; the launch traced here: 80.6 us
  Pallas kernels  72.1 us (89%)
  local copies, waits for them, and re-layouts  6.07 us (8%)
  between operations  2.47 us (3%)
    pallas_call x1, Pallas kernels, shards(): pl.pallas_call(functools.partial(chain_kernel, n), out_shape=(jax.ShapeDt...  55.6 us
    pallas_call x1, Pallas kernels, shards(): pl.pallas_call(maps_kernel, out_shape=(jax.ShapeDtypeStruct((N, N), jnp.b...  16.5 us
    unnamed x15, local copies, waits for them, and re-layouts  6.07 us

profile of v1, /device:TPU:0, one launch (start us, length us, event | category | flops | bytes accessed | tf_op | source)
XLA Modules:
  0.0 80.6 jit_solution(3131401532492226531)
XLA Ops:
  1.3 0.0 copy-start
  1.3 1.6 %copy-done = bf16[1024,1024]{1,0:T(8,128)(2,1)S(1)} copy-done((bf16[1024,1024]{1,0:T(8,128)(2,1)S(1)}, bf16[1024,1024]{1,0:T(8,128)(2,1)}, u32[]{:S(2)}) %copy-start) | copy-done | bytes 2097176
  2.9 0.0 copy-start.1
  2.9 0.9 %copy-done.1 = bf16[1024,128]{1,0:T(8,128)(2,1)S(1)} copy-done((bf16[1024,128]{1,0:T(8,128)(2,1)S(1)}, bf16[1024,128]{1,0:T(8,128)(2,1)}, u32[]{:S(2)}) %copy-start.1) | copy-done | bytes 262168
  3.8 0.0 copy-start.2
  3.8 0.9 %copy-done.2 = bf16[1,256,256]{2,1,0:T(8,128)(2,1)S(1)} copy-done((bf16[1,256,256]{2,1,0:T(8,128)(2,1)S(1)}, bf16[1,256,256]{2,1,0:T(8,128)(2,1)}, u32[]{:S(2)}) %copy-start.2) | copy-done | bytes 131096
  4.7 0.0 copy-start.4
  4.7 0.7 copy-done.4
  5.4 0.0 copy-start.5
  5.4 0.7 copy-done.5
  6.1 0.0 copy-start.6
  6.1 0.7 copy-done.6
  6.8 0.0 copy-start.3
  6.8 16.5 %maps.1 = (bf16[1024,1024]{1,0:T(8,128)(2,1)S(1)}, f32[1,1024]{1,0:T(1,128)S(1)}, f32[256,1024]{1,0:T(8,128)S(1)}, f32[128,256]{1,0:T(8,128)S(1)}, f32[256,128]{...) custom-call(s32[1,2,2]{2,1,0:T(2,128)S(1)} %copy-done.4, s32[1]{0:T(128)S(6)} %copy.12.count, ...), custom_call_target="tpu_custom_call" | custom-call | tf_op jit(solution)/shard_map/maps/pallas_call | solution.py:201
  23.3 0.0 copy-done.3
  23.3 55.6 %chain.1 = (f32[1,1024]{1,0:T(1,128)S(1)}, f32[1,128]{1,0:T(1,128)S(1)}) custom-call(s32[1]{0:T(128)S(6)} %copy.12.count, bf16[1024,1024]{1,0:T(8,128)(2,1)S(1)} %get-tuple-element.11.transit, f32[1,1024]{1,0:T(1,128)S(1)} %get-tuple-element.12.offset, f32[256,1024]{1,0:T(8,128)S(1)} %get-tuple-element.13.forward, f32[128,256]{1,0:T(8,128)S(1)} %get-tuple-element.14.gain, ...), custom_call_target="tpu_custom_call" | custom-call | tf_op jit(solution)/shard_map/chain/pallas_call | solution.py:218
  78.9 0.6 copy.13
Async XLA Ops:
  1.3 1.6 %copy-start = (bf16[1024,1024]{1,0:T(8,128)(2,1)S(1)}, bf16[1024,1024]{1,0:T(8,128)(2,1)}, u32[]{:S(2)}) copy-start(bf16[1024,1024]{1,0:T(8,128)(2,1)} %trans.1) | copy-start | bytes 6291460
  2.9 0.9 %copy-start.1 = (bf16[1024,128]{1,0:T(8,128)(2,1)S(1)}, bf16[1024,128]{1,0:T(8,128)(2,1)}, u32[]{:S(2)}) copy-start(bf16[1024,128]{1,0:T(8,128)(2,1)} %ensemble.1) | copy-start | bytes 786436
  3.8 0.9 %copy-start.2 = (bf16[1,256,256]{2,1,0:T(8,128)(2,1)S(1)}, bf16[1,256,256]{2,1,0:T(8,128)(2,1)}, u32[]{:S(2)}) copy-start(bf16[1,256,256]{2,1,0:T(8,128)(2,1)} %hrows.1) | copy-start | bytes 393220
  4.7 0.7 copy-start.4
  5.4 0.7 copy-start.5
  6.1 0.7 copy-start.6
  6.8 16.5 %copy-start.3 = (f32[1024]{0:T(1024)S(1)}, f32[1024]{0:T(1024)}, u32[]{:S(2)}) copy-start(f32[1024]{0:T(1024)} %param.15) | copy-start | bytes 12292

commit v2 on v1

v2 whole, which is shorter than its diff:
```python
import functools

import jax
import jax.numpy as jnp
from jax import lax
from jax.experimental import pallas as pl
from jax.experimental.pallas import tpu as pltpu
from jax.sharding import PartitionSpec as P

N = 1024
BLK = 128
NB = 8
MB = 2
KB = 2
MOBS = 256
NE = 128
HIGH = lax.Precision.HIGHEST
VMEM = pl.BlockSpec(memory_space=pltpu.VMEM)
SMEM = pl.BlockSpec(memory_space=pltpu.SMEM)


def times(left, right, precision=None):
    return lax.dot_general(
        left, right, (((1,), (0,)), ((), ())), precision=precision, preferred_element_type=jnp.float32
    )


def times_t(left, right, precision=None):
    return lax.dot_general(
        left, right, (((1,), (1,)), ((), ())), precision=precision, preferred_element_type=jnp.float32
    )


def split_rows(vector):
    high = vector.astype(jnp.bfloat16).astype(jnp.float32)
    rest = vector - high
    middle = rest.astype(jnp.bfloat16).astype(jnp.float32)
    lowest = rest - middle
    row = lax.broadcasted_iota(jnp.int32, (16, N), 0)
    stacked = jnp.where(row == 0, high, jnp.where(row == 1, middle, jnp.where(row == 2, lowest, 0.0)))
    return stacked.astype(jnp.bfloat16)


def apply_rows(matrix, vector):
    return jnp.sum(times_t(split_rows(vector), matrix), axis=0, keepdims=True)


def observe_kernel(
    pattern, count, trans_hbm, ensemble, hrows, yobs, rvar,
    reduced, offset, forward, gain, member, dinv_out, masked_out,
    trans, swept, trans_sem,
):
    fetch = pltpu.make_async_copy(trans_hbm, trans, trans_sem)
    fetch.start()
    live = count[0]
    rows = lax.broadcasted_iota(jnp.int32, (MOBS, 1), 0)
    active_rows = (rows < live).astype(jnp.float32)
    lanes = lax.broadcasted_iota(jnp.int32, (1, MOBS), 1)
    active_lanes = (lanes < live).astype(jnp.float32)
    for m in range(MB):
        here = pl.ds(m * BLK, BLK)
        starts = [pl.multiple_of(pattern[0, m, k] * BLK, BLK) for k in range(KB)]
        ecols = jnp.concatenate([ensemble[pl.ds(s, BLK), :] for s in starts], axis=0)
        alive = active_rows[m * BLK : (m + 1) * BLK]
        member[here, :] = times(hrows[0, here, :], ecols) * alive
    dinv = active_lanes / rvar[...]
    masked = yobs[...] * active_lanes
    scaled = member[...].T * dinv
    row = lax.broadcasted_iota(jnp.int32, (NE, NE), 0)
    lane = lax.broadcasted_iota(jnp.int32, (NE, NE), 1)
    begin = times(scaled, member[...], HIGH) / NE + (row == lane).astype(jnp.float32)
    swept[...] = (begin + begin.T) * 0.5

    def sweep(k, carry):
        x = swept[...]
        r = swept[pl.ds(k, 1), :]
        on_lane = lane == k
        on_row = row == k
        c = jnp.sum(jnp.where(on_lane, x, 0.0), axis=1, keepdims=True)
        one_lane = lax.broadcasted_iota(jnp.int32, (1, NE), 1) == k
        pivot = jnp.sum(jnp.where(one_lane, r, 0.0), axis=1, keepdims=True)
        inv = 1.0 / pivot
        scaled_r = jnp.where(one_lane, -inv, r * inv)
        out = jnp.where(on_lane, c * inv, x - c * scaled_r)
        swept[...] = jnp.where(on_row, scaled_r, out)
        return carry

    lax.fori_loop(0, NE, sweep, 0)
    gains = times(-swept[...], scaled, HIGH) / NE
    seen = jnp.broadcast_to(masked, (8, MOBS))
    weights = times_t(seen, gains, HIGH)
    gain[...] = gains
    dinv_out[...] = dinv
    masked_out[...] = masked
    offset[...] = times_t(weights, ensemble[...].astype(jnp.float32), HIGH)[:1]

    fetch.wait()
    for m in range(MB):
        here = pl.ds(m * BLK, BLK)
        starts = [pl.multiple_of(pattern[0, m, k] * BLK, BLK) for k in range(KB)]
        fcols = jnp.concatenate([trans[pl.ds(s, BLK), :] for s in starts], axis=0)
        alive = active_rows[m * BLK : (m + 1) * BLK]
        forward[here, :] = times(hrows[0, here, :], fcols) * alive
    reduced[...] = times(gains, forward[...], HIGH).astype(jnp.bfloat16)


def chain_kernel(
    n, count, trans_hbm, ensemble, reduced, offset, forward, gain, member, dinv_in, masked, first,
    states, misfit,
    trans, transit, earlier, step, reduced_in,
    offset_in, step_offset, incoming, current, produced, tiles,
    trans_sem, pair_send, pair_recv, hop_send, hop_recv, tile_send, tile_recv,
):
    me = lax.axis_index("tm")
    odd = lax.rem(me, 2) == 1
    even = lax.rem(me, 2) == 0
    fetch = pltpu.make_async_copy(trans_hbm, trans, trans_sem)
    fetch.start()
    barrier = pltpu.get_barrier_semaphore()

    def greet(i, carry):
        pl.semaphore_signal(barrier, inc=1, device_id={"tm": lax.rem(me + i, n)})
        return carry

    lax.fori_loop(1, n, greet, 0)
    pl.semaphore_wait(barrier, n - 1)
    after_me = lax.rem(me + 1, n)
    after_that = lax.rem(me + 2, n)
    give_matrix = pltpu.make_async_remote_copy(
        src_ref=reduced, dst_ref=reduced_in, send_sem=pair_send.at[0], recv_sem=pair_recv.at[0],
        device_id={"tm": after_me},
    )
    give_offset = pltpu.make_async_remote_copy(
        src_ref=offset, dst_ref=offset_in, send_sem=pair_send.at[1], recv_sem=pair_recv.at[1],
        device_id={"tm": after_me},
    )
    far = pltpu.make_async_remote_copy(
        src_ref=produced, dst_ref=incoming, send_sem=hop_send.at[0], recv_sem=hop_recv,
        device_id={"tm": after_that},
    )
    near = pltpu.make_async_remote_copy(
        src_ref=produced, dst_ref=incoming, send_sem=hop_send.at[1], recv_sem=hop_recv,
        device_id={"tm": after_me},
    )

    @pl.when(even)
    def _():
        give_matrix.start()
        give_offset.start()

    fetch.wait()

    def transit_of(low_rank):
        return (trans[...].astype(jnp.float32) - times(ensemble[...], low_rank)).astype(jnp.bfloat16)

    @pl.when(even)
    def _():
        step[...] = transit_of(reduced[...])
        step_offset[...] = offset[...]

    @pl.when(odd)
    def _():
        transit[...] = transit_of(reduced[...])
        give_matrix.wait_recv()
        give_offset.wait_recv()
        earlier[...] = transit_of(reduced_in[...])

        def product(i, carry):
            columns = pl.ds(pl.multiple_of(i * 256, 256), 256)
            step[:, columns] = times(transit[...], earlier[:, columns]).astype(jnp.bfloat16)
            return carry

        lax.fori_loop(0, N // 256, product, 0)
        step_offset[...] = apply_rows(transit[...], offset_in[...]) + offset[...]

    @pl.when(me < 2)
    def _():
        current[...] = first[...]

    @pl.when(me >= 2)
    def _():
        near.wait_recv()
        current[...] = incoming[...]

    produced[...] = apply_rows(step[...], current[...]) + step_offset[...]
    sends = jnp.logical_and(odd, me < n - 1)

    @pl.when(sends)
    def _():
        far.start()
        near.start()

    states[...] = produced[...]

    @pl.when(odd)
    def _():
        current[...] = apply_rows(earlier[...], current[...]) + offset_in[...]

    seen = jnp.broadcast_to(masked[...], (8, MOBS))
    innovation = seen - times_t(jnp.broadcast_to(current[...], (8, N)), forward[...], HIGH)
    moved = times_t(innovation, gain[...], HIGH)
    left = innovation - times_t(moved, member[...], HIGH)
    fit = jnp.sum(left * left * dinv_in[...], axis=1, keepdims=True) + NE * jnp.sum(
        moved * moved, axis=1, keepdims=True
    )
    tile_lane = lax.broadcasted_iota(jnp.int32, (8, NE), 1)
    tiles[me] = jnp.where(tile_lane == 0, fit, count[0].astype(jnp.float32))

    def tell(i):
        return pltpu.make_async_remote_copy(
            src_ref=tiles.at[me],
            dst_ref=tiles.at[me],
            send_sem=tile_send.at[i],
            recv_sem=tile_recv.at[me],
            device_id={"tm": lax.rem(me + i, n)},
        )

    def hear(i):
        other = lax.rem(me + n - i, n)
        return pltpu.make_async_remote_copy(
            src_ref=tiles.at[other],
            dst_ref=tiles.at[other],
            send_sem=tile_send.at[i],
            recv_sem=tile_recv.at[other],
            device_id={"tm": other},
        )

    def start(i, carry):
        tell(i).start()
        return carry

    def finish(i, carry):
        hear(i).wait_recv()
        return carry

    def sent(i, carry):
        tell(i).wait_send()
        return carry

    lax.fori_loop(1, n, start, 0)
    lax.fori_loop(1, n, finish, 0)
    lax.fori_loop(1, n, sent, 0)

    @pl.when(even)
    def _():
        give_matrix.wait_send()
        give_offset.wait_send()

    @pl.when(sends)
    def _():
        far.wait_send()
        near.wait_send()

    total = jnp.sum(tiles[...], axis=0)[:1]
    one = lax.broadcasted_iota(jnp.int32, (1, NE), 1)
    fits = jnp.sum(jnp.where(one == 0, total, 0.0), axis=1, keepdims=True)
    lives = jnp.sum(jnp.where(one == 1, total, 0.0), axis=1, keepdims=True)
    misfit[...] = jnp.broadcast_to(fits / lives, (1, NE))


def shards(
    n, trans_matrix, ensemble, obs_operator, pattern, counts, observations, obs_variance, initial_state
):
    f32, bf16 = jnp.float32, jnp.bfloat16
    hbm = pl.BlockSpec(memory_space=pltpu.HBM)
    observed = pl.pallas_call(
        observe_kernel,
        out_shape=(
            jax.ShapeDtypeStruct((NE, N), bf16),
            jax.ShapeDtypeStruct((1, N), f32),
            jax.ShapeDtypeStruct((MOBS, N), f32),
            jax.ShapeDtypeStruct((NE, MOBS), f32),
            jax.ShapeDtypeStruct((MOBS, NE), f32),
            jax.ShapeDtypeStruct((1, MOBS), f32),
            jax.ShapeDtypeStruct((1, MOBS), f32),
        ),
        in_specs=[SMEM, SMEM, hbm] + [VMEM] * 4,
        out_specs=(VMEM,) * 7,
        scratch_shapes=[
            pltpu.VMEM((N, N), bf16),
            pltpu.VMEM((NE, NE), f32),
            pltpu.SemaphoreType.DMA,
        ],
        compiler_params=pltpu.CompilerParams(vmem_limit_bytes=32 * 1024 * 1024),
        name="observe",
    )(pattern, counts, trans_matrix, ensemble, obs_operator, observations, obs_variance)
    states, misfit = pl.pallas_call(
        functools.partial(chain_kernel, n),
        out_shape=(jax.ShapeDtypeStruct((1, N), f32), jax.ShapeDtypeStruct((1, NE), f32)),
        in_specs=[SMEM, hbm] + [VMEM] * 9,
        out_specs=(VMEM, VMEM),
        scratch_shapes=[
            pltpu.VMEM((N, N), bf16),
            pltpu.VMEM((N, N), bf16),
            pltpu.VMEM((N, N), bf16),
            pltpu.VMEM((N, N), bf16),
            pltpu.VMEM((NE, N), bf16),
            pltpu.VMEM((1, N), f32),
            pltpu.VMEM((1, N), f32),
            pltpu.VMEM((1, N), f32),
            pltpu.VMEM((1, N), f32),
            pltpu.VMEM((1, N), f32),
            pltpu.VMEM((n, 8, NE), f32),
            pltpu.SemaphoreType.DMA,
            pltpu.SemaphoreType.DMA((2,)),
            pltpu.SemaphoreType.DMA((2,)),
            pltpu.SemaphoreType.DMA((2,)),
            pltpu.SemaphoreType.DMA,
            pltpu.SemaphoreType.DMA((n,)),
            pltpu.SemaphoreType.DMA((n,)),
        ],
        compiler_params=pltpu.CompilerParams(
            collective_id=0, has_side_effects=True, vmem_limit_bytes=40 * 1024 * 1024
        ),
        name="chain",
    )(counts, trans_matrix, ensemble, *observed, initial_state.reshape(1, N))
    return states, misfit[0, :1]


def solution(mesh):
    return jax.shard_map(
        functools.partial(shards, mesh.shape["tm"]),
        mesh=mesh,
        in_specs=(
            P(),
            P(),
            P(("groups", "tm"), None, None),
            P(("groups", "tm"), None, None),
            P(("groups", "tm")),
            P(("groups", "tm"), None),
            P(("groups", "tm"), None),
            P("groups"),
        ),
        out_specs=(P(("groups", "tm"), None), P("groups")),
        check_vma=False,
    )
```

time: 80.9 us -> 63.1 us (0.78)
  Pallas kernels: 72.1 us -> 54.3 us
    pallas_call x1, Pallas kernels: 55.6 us -> 37.7 us  [shards(): pl.pallas_call(functools.partial(chain_kernel, n), out_shape=(jax.ShapeDt...]
    unnamed x15 -> x19, local copies, waits for them, and re-layouts: 6.07 us -> 6.08 us
where the time goes in v2:
time: 63.1 us; the launch traced here: 62.8 us
  Pallas kernels  54.3 us (86%)
  local copies, waits for them, and re-layouts  6.08 us (10%)
  between operations  2.5 us (4%)
    pallas_call x1, Pallas kernels, shards(): pl.pallas_call(functools.partial(chain_kernel, n), out_shape=(jax.ShapeDt...  37.7 us
    pallas_call x1, Pallas kernels, shards(): pl.pallas_call(observe_kernel, out_shape=(jax.ShapeDtypeStruct((NE, N), b...  16.5 us
    unnamed x19, local copies, waits for them, and re-layouts  6.08 us

profile of v2, /device:TPU:0, one launch (start us, length us, event | category | flops | bytes accessed | tf_op | source)
XLA Modules:
  0.0 62.8 jit_solution(1685845310877024074)
XLA Ops:
  1.3 0.0 copy-start
  1.3 1.6 %copy-done = bf16[1024,1024]{1,0:T(8,128)(2,1)S(1)} copy-done((bf16[1024,1024]{1,0:T(8,128)(2,1)S(1)}, bf16[1024,1024]{1,0:T(8,128)(2,1)}, u32[]{:S(2)}) %copy-start) | copy-done | bytes 2097176
  2.9 0.0 copy-start.2
  2.9 0.9 %copy-done.2 = bf16[1024,128]{1,0:T(8,128)(2,1)S(1)} copy-done((bf16[1024,128]{1,0:T(8,128)(2,1)S(1)}, bf16[1024,128]{1,0:T(8,128)(2,1)}, u32[]{:S(2)}) %copy-start.2) | copy-done | bytes 262168
  3.8 0.0 copy-start.4
  3.8 0.9 %copy-done.4 = bf16[1,256,256]{2,1,0:T(8,128)(2,1)S(1)} copy-done((bf16[1,256,256]{2,1,0:T(8,128)(2,1)S(1)}, bf16[1,256,256]{2,1,0:T(8,128)(2,1)}, u32[]{:S(2)}) %copy-start.4) | copy-done | bytes 131096
  4.7 0.0 copy-start.6
  4.7 0.7 %copy-done.6 = s32[1,2,2]{2,1,0:T(2,128)S(1)} copy-done((s32[1,2,2]{2,1,0:T(2,128)S(1)}, s32[1,2,2]{2,1,0:T(2,128)}, u32[]{:S(2)}) %copy-start.6) | copy-done | bytes 40
  5.4 0.0 copy-start.7
  5.4 0.7 %copy-done.7 = f32[1,256]{1,0:T(1,128)S(1)} copy-done((f32[1,256]{1,0:T(1,128)S(1)}, f32[1,256]{1,0:T(1,128)}, u32[]{:S(2)}) %copy-start.7) | copy-done | bytes 1048
  6.1 0.0 copy-start.8
  6.1 0.7 %copy-done.8 = f32[1,256]{1,0:T(1,128)S(1)} copy-done((f32[1,256]{1,0:T(1,128)S(1)}, f32[1,256]{1,0:T(1,128)}, u32[]{:S(2)}) %copy-start.8) | copy-done | bytes 1048
  6.8 0.0 copy-start.1
  6.8 0.0 copy-start.3
  6.8 0.0 copy-start.5
  6.8 16.5 %observe.1 = (bf16[128,1024]{1,0:T(8,128)(2,1)S(1)}, f32[1,1024]{1,0:T(1,128)S(1)}, f32[256,1024]{1,0:T(8,128)S(1)}, f32[128,256]{1,0:T(8,128)S(1)}, f32[256,128...) custom-call(s32[1,2,2]{2,1,0:T(2,128)S(1)} %copy-done.6, s32[1]{0:T(128)S(6)} %copy.12.count, ...), custom_call_target="tpu_custom_call" | custom-call | tf_op jit(solution)/shard_map/observe/pallas_call | solution.py:266
  23.3 0.0 copy-done.1
  23.3 0.0 copy-done.3
  23.3 0.0 copy-done.5
  23.3 37.7 %chain.1 = (f32[1,1024]{1,0:T(1,128)S(1)}, f32[1,128]{1,0:T(1,128)S(1)}) custom-call(s32[1]{0:T(128)S(6)} %copy.12.count, bf16[1024,1024]{1,0:T(8,128)(2,1)S(1)} %copy-done.1, bf16[1024,128]{1,0:T(8,128)(2,1)S(1)} %copy-done.3, bf16[128,1024]{1,0:T(8,128)(2,1)S(1)} %get-tuple-element.11.reduced, f32[1,1024]{1,0:T(1,128)S(1)} %get-tuple-element.12.offset, ...), custom_call_target="tpu_custom_call" | custom-call | tf_op jit(solution)/shard_map/chain/pallas_call | solution.py:287
  61.1 0.6 copy.13
Async XLA Ops:
  1.3 1.6 %copy-start = (bf16[1024,1024]{1,0:T(8,128)(2,1)S(1)}, bf16[1024,1024]{1,0:T(8,128)(2,1)}, u32[]{:S(2)}) copy-start(bf16[1024,1024]{1,0:T(8,128)(2,1)} %trans_hbm.3) | copy-start | bytes 6291460
  2.9 0.9 %copy-start.2 = (bf16[1024,128]{1,0:T(8,128)(2,1)S(1)}, bf16[1024,128]{1,0:T(8,128)(2,1)}, u32[]{:S(2)}) copy-start(bf16[1024,128]{1,0:T(8,128)(2,1)} %ensemble.3) | copy-start | bytes 786436
  3.8 0.9 %copy-start.4 = (bf16[1,256,256]{2,1,0:T(8,128)(2,1)S(1)}, bf16[1,256,256]{2,1,0:T(8,128)(2,1)}, u32[]{:S(2)}) copy-start(bf16[1,256,256]{2,1,0:T(8,128)(2,1)} %hrows.1) | copy-start | bytes 393220
  4.7 0.7 %copy-start.6 = (s32[1,2,2]{2,1,0:T(2,128)S(1)}, s32[1,2,2]{2,1,0:T(2,128)}, u32[]{:S(2)}) copy-start(s32[1,2,2]{2,1,0:T(2,128)} %pattern.1) | copy-start | bytes 52
  5.4 0.7 %copy-start.7 = (f32[1,256]{1,0:T(1,128)S(1)}, f32[1,256]{1,0:T(1,128)}, u32[]{:S(2)}) copy-start(f32[1,256]{1,0:T(1,128)} %yobs.1) | copy-start | bytes 3076
  6.1 0.7 %copy-start.8 = (f32[1,256]{1,0:T(1,128)S(1)}, f32[1,256]{1,0:T(1,128)}, u32[]{:S(2)}) copy-start(f32[1,256]{1,0:T(1,128)} %rvar.1) | copy-start | bytes 3076
  6.8 16.5 %copy-start.1 = (bf16[1024,1024]{1,0:T(8,128)(2,1)S(1)}, bf16[1024,1024]{1,0:T(8,128)(2,1)}, u32[]{:S(2)}) copy-start(bf16[1024,1024]{1,0:T(8,128)(2,1)} %trans_hbm.3) | copy-start | bytes 6291460
  6.8 16.6 %copy-start.3 = (bf16[1024,128]{1,0:T(8,128)(2,1)S(1)}, bf16[1024,128]{1,0:T(8,128)(2,1)}, u32[]{:S(2)}) copy-start(bf16[1024,128]{1,0:T(8,128)(2,1)} %ensemble.3) | copy-start | bytes 786436
  6.8 16.6 %copy-start.5 = (f32[1024]{0:T(1024)S(1)}, f32[1024]{0:T(1024)}, u32[]{:S(2)}) copy-start(f32[1024]{0:T(1024)} %param.15) | copy-start | bytes 12292

commit v3 on v2

--- a/solution.py
+++ b/solution.py
@@ -71,21 +71,32 @@
     begin = times(scaled, member[...], HIGH) / NE + (row == lane).astype(jnp.float32)
     swept[...] = (begin + begin.T) * 0.5
 
-    def sweep(k, carry):
+    one_lane = lax.broadcasted_iota(jnp.int32, (1, NE), 1)
+
+    def pick(vector, k):
+        return jnp.sum(jnp.where(one_lane == k, vector, 0.0), axis=1, keepdims=True)
+
+    def sweep(j, carry):
+        k = 2 * j
         x = swept[...]
-        r = swept[pl.ds(k, 1), :]
-        on_lane = lane == k
-        on_row = row == k
-        c = jnp.sum(jnp.where(on_lane, x, 0.0), axis=1, keepdims=True)
-        one_lane = lax.broadcasted_iota(jnp.int32, (1, NE), 1) == k
-        pivot = jnp.sum(jnp.where(one_lane, r, 0.0), axis=1, keepdims=True)
-        inv = 1.0 / pivot
-        scaled_r = jnp.where(one_lane, -inv, r * inv)
-        out = jnp.where(on_lane, c * inv, x - c * scaled_r)
-        swept[...] = jnp.where(on_row, scaled_r, out)
-        return carry
-
-    lax.fori_loop(0, NE, sweep, 0)
+        r0 = swept[pl.ds(k, 1), :]
+        r1 = swept[pl.ds(k + 1, 1), :]
+        c0 = jnp.sum(jnp.where(lane == k, x, 0.0), axis=1, keepdims=True)
+        c1 = jnp.sum(jnp.where(lane == k + 1, x, 0.0), axis=1, keepdims=True)
+        a, b, d = pick(r0, k), pick(r0, k + 1), pick(r1, k + 1)
+        ra = 1.0 / a
+        g = b * ra
+        e = 1.0 / (d - b * g)
+        ge = -g * e
+        aa = ra - g * ge
+        s0 = jnp.where(one_lane == k, -aa, jnp.where(one_lane == k + 1, -ge, aa * r0 + ge * r1))
+        s1 = jnp.where(one_lane == k, -ge, jnp.where(one_lane == k + 1, -e, ge * r0 + e * r1))
+        inside = jnp.logical_or(lane == k, lane == k + 1)
+        out = jnp.where(inside, 0.0, x) - c0 * s0 - c1 * s1
+        swept[...] = jnp.where(row == k, s0, jnp.where(row == k + 1, s1, out))
+        return carry
+
+    lax.fori_loop(0, NE // 2, sweep, 0)
     gains = times(-swept[...], scaled, HIGH) / NE
     seen = jnp.broadcast_to(masked, (8, MOBS))
     weights = times_t(seen, gains, HIGH)
@@ -155,7 +166,13 @@
 
     @pl.when(even)
     def _():
-        step[...] = transit_of(reduced[...])
+        def turned(i, carry):
+            here = pl.ds(pl.multiple_of(i * 256, 256), 256)
+            block = trans[here, :].astype(jnp.float32) - times(ensemble[here, :], reduced[...])
+            step[:, here] = block.T.astype(jnp.bfloat16)
+            return carry
+
+        lax.fori_loop(0, N // 256, turned, 0)
         step_offset[...] = offset[...]
 
     @pl.when(odd)
@@ -167,7 +184,7 @@
 
         def product(i, carry):
             columns = pl.ds(pl.multiple_of(i * 256, 256), 256)
-            step[:, columns] = times(transit[...], earlier[:, columns]).astype(jnp.bfloat16)
+            step[columns, :] = times(transit[...], earlier[:, columns]).T.astype(jnp.bfloat16)
             return carry
 
         lax.fori_loop(0, N // 256, product, 0)
@@ -182,7 +199,8 @@
         near.wait_recv()
         current[...] = incoming[...]
 
-    produced[...] = apply_rows(step[...], current[...]) + step_offset[...]
+    parts = times(split_rows(current[...]), step[...])
+    produced[...] = jnp.sum(parts, axis=0, keepdims=True) + step_offset[...]
     sends = jnp.logical_and(odd, me < n - 1)
 
     @pl.when(sends)

time: 63.1 us -> 56.5 us (0.90)
  Pallas kernels: 54.3 us -> 47.6 us
    pallas_call x1, Pallas kernels: 16.5 us -> 11.4 us  [shards(): pl.pallas_call(observe_kernel, out_shape=(jax.ShapeDtypeStruct((NE, N), b...]
    pallas_call x1, Pallas kernels: 37.7 us -> 36.2 us  [shards(): pl.pallas_call(functools.partial(chain_kernel, n), out_shape=(jax.ShapeDt...]
where the time goes in v3:
time: 56.5 us; the launch traced here: 56.2 us
  Pallas kernels  47.6 us (84%)
  local copies, waits for them, and re-layouts  6.08 us (11%)
  between operations  2.5 us (4%)
    pallas_call x1, Pallas kernels, shards(): pl.pallas_call(functools.partial(chain_kernel, n), out_shape=(jax.ShapeDt...  36.2 us
    pallas_call x1, Pallas kernels, shards(): pl.pallas_call(observe_kernel, out_shape=(jax.ShapeDtypeStruct((NE, N), b...  11.4 us
    unnamed x19, local copies, waits for them, and re-layouts  6.08 us

profile of v3, /device:TPU:0, one launch (start us, length us, event | category | flops | bytes accessed | tf_op | source)
XLA Modules:
  0.0 56.2 jit_solution(3583894379015253696)
XLA Ops:
  1.3 0.0 copy-start
  1.3 1.6 %copy-done = bf16[1024,1024]{1,0:T(8,128)(2,1)S(1)} copy-done((bf16[1024,1024]{1,0:T(8,128)(2,1)S(1)}, bf16[1024,1024]{1,0:T(8,128)(2,1)}, u32[]{:S(2)}) %copy-start) | copy-done | bytes 2097176
  2.9 0.0 copy-start.2
  2.9 0.9 %copy-done.2 = bf16[1024,128]{1,0:T(8,128)(2,1)S(1)} copy-done((bf16[1024,128]{1,0:T(8,128)(2,1)S(1)}, bf16[1024,128]{1,0:T(8,128)(2,1)}, u32[]{:S(2)}) %copy-start.2) | copy-done | bytes 262168
  3.8 0.0 copy-start.4
  3.8 0.9 %copy-done.4 = bf16[1,256,256]{2,1,0:T(8,128)(2,1)S(1)} copy-done((bf16[1,256,256]{2,1,0:T(8,128)(2,1)S(1)}, bf16[1,256,256]{2,1,0:T(8,128)(2,1)}, u32[]{:S(2)}) %copy-start.4) | copy-done | bytes 131096
  4.7 0.0 copy-start.6
  4.7 0.7 %copy-done.6 = s32[1,2,2]{2,1,0:T(2,128)S(1)} copy-done((s32[1,2,2]{2,1,0:T(2,128)S(1)}, s32[1,2,2]{2,1,0:T(2,128)}, u32[]{:S(2)}) %copy-start.6) | copy-done | bytes 40
  5.4 0.0 copy-start.7
  5.4 0.7 %copy-done.7 = f32[1,256]{1,0:T(1,128)S(1)} copy-done((f32[1,256]{1,0:T(1,128)S(1)}, f32[1,256]{1,0:T(1,128)}, u32[]{:S(2)}) %copy-start.7) | copy-done | bytes 1048
  6.1 0.0 copy-start.8
  6.1 0.7 %copy-done.8 = f32[1,256]{1,0:T(1,128)S(1)} copy-done((f32[1,256]{1,0:T(1,128)S(1)}, f32[1,256]{1,0:T(1,128)}, u32[]{:S(2)}) %copy-start.8) | copy-done | bytes 1048
  6.8 0.0 copy-start.1
  6.8 0.0 copy-start.3
  6.8 0.0 copy-start.5
  6.8 11.4 %observe.1 = (bf16[128,1024]{1,0:T(8,128)(2,1)S(1)}, f32[1,1024]{1,0:T(1,128)S(1)}, f32[256,1024]{1,0:T(8,128)S(1)}, f32[128,256]{1,0:T(8,128)S(1)}, f32[256,128...) custom-call(s32[1,2,2]{2,1,0:T(2,128)S(1)} %copy-done.6, s32[1]{0:T(128)S(6)} %copy.12.count, ...), custom_call_target="tpu_custom_call" | custom-call | tf_op jit(solution)/shard_map/observe/pallas_call | solution.py:284
  18.2 0.0 copy-done.1
  18.2 0.0 copy-done.3
  18.2 0.0 copy-done.5
  18.2 36.2 %chain.1 = (f32[1,1024]{1,0:T(1,128)S(1)}, f32[1,128]{1,0:T(1,128)S(1)}) custom-call(s32[1]{0:T(128)S(6)} %copy.12.count, bf16[1024,1024]{1,0:T(8,128)(2,1)S(1)} %copy-done.1, bf16[1024,128]{1,0:T(8,128)(2,1)S(1)} %copy-done.3, bf16[128,1024]{1,0:T(8,128)(2,1)S(1)} %get-tuple-element.11.reduced, f32[1,1024]{1,0:T(1,128)S(1)} %get-tuple-element.12.offset, ...), custom_call_target="tpu_custom_call" | custom-call | tf_op jit(solution)/shard_map/chain/pallas_call | solution.py:305
  54.4 0.6 %copy.13 = f32[1,1024]{1,0:T(1,128)} copy(f32[1,1024]{1,0:T(1,128)S(1)} %get-tuple-element.22) | data formatting | bytes 8192
Async XLA Ops:
  1.3 1.6 %copy-start = (bf16[1024,1024]{1,0:T(8,128)(2,1)S(1)}, bf16[1024,1024]{1,0:T(8,128)(2,1)}, u32[]{:S(2)}) copy-start(bf16[1024,1024]{1,0:T(8,128)(2,1)} %trans_hbm.3) | copy-start | bytes 6291460
  2.9 0.9 %copy-start.2 = (bf16[1024,128]{1,0:T(8,128)(2,1)S(1)}, bf16[1024,128]{1,0:T(8,128)(2,1)}, u32[]{:S(2)}) copy-start(bf16[1024,128]{1,0:T(8,128)(2,1)} %ensemble.3) | copy-start | bytes 786436
  3.8 0.9 %copy-start.4 = (bf16[1,256,256]{2,1,0:T(8,128)(2,1)S(1)}, bf16[1,256,256]{2,1,0:T(8,128)(2,1)}, u32[]{:S(2)}) copy-start(bf16[1,256,256]{2,1,0:T(8,128)(2,1)} %hrows.1) | copy-start | bytes 393220
  4.7 0.7 %copy-start.6 = (s32[1,2,2]{2,1,0:T(2,128)S(1)}, s32[1,2,2]{2,1,0:T(2,128)}, u32[]{:S(2)}) copy-start(s32[1,2,2]{2,1,0:T(2,128)} %pattern.1) | copy-start | bytes 52
  5.4 0.7 %copy-start.7 = (f32[1,256]{1,0:T(1,128)S(1)}, f32[1,256]{1,0:T(1,128)}, u32[]{:S(2)}) copy-start(f32[1,256]{1,0:T(1,128)} %yobs.1) | copy-start | bytes 3076
  6.1 0.7 %copy-start.8 = (f32[1,256]{1,0:T(1,128)S(1)}, f32[1,256]{1,0:T(1,128)}, u32[]{:S(2)}) copy-start(f32[1,256]{1,0:T(1,128)} %rvar.1) | copy-start | bytes 3076
  6.8 11.5 %copy-start.1 = (bf16[1024,1024]{1,0:T(8,128)(2,1)S(1)}, bf16[1024,1024]{1,0:T(8,128)(2,1)}, u32[]{:S(2)}) copy-start(bf16[1024,1024]{1,0:T(8,128)(2,1)} %trans_hbm.3) | copy-start | bytes 6291460
  6.8 11.5 %copy-start.3 = (bf16[1024,128]{1,0:T(8,128)(2,1)S(1)}, bf16[1024,128]{1,0:T(8,128)(2,1)}, u32[]{:S(2)}) copy-start(bf16[1024,128]{1,0:T(8,128)(2,1)} %ensemble.3) | copy-start | bytes 786436
  6.8 11.5 %copy-start.5 = (f32[1024]{0:T(1024)S(1)}, f32[1024]{0:T(1024)}, u32[]{:S(2)}) copy-start(f32[1024]{0:T(1024)} %param.15) | copy-start | bytes 12292

commit v4 on v3

--- a/solution.py
+++ b/solution.py
@@ -125,6 +125,8 @@
     me = lax.axis_index("tm")
     odd = lax.rem(me, 2) == 1
     even = lax.rem(me, 2) == 0
+    in_turn = jnp.logical_and(odd, me < 4)
+    composed = jnp.logical_and(odd, me >= 4)
     fetch = pltpu.make_async_copy(trans_hbm, trans, trans_sem)
     fetch.start()
     barrier = pltpu.get_barrier_semaphore()
@@ -182,6 +184,8 @@
         give_offset.wait_recv()
         earlier[...] = transit_of(reduced_in[...])
 
+    @pl.when(composed)
+    def _():
         def product(i, carry):
             columns = pl.ds(pl.multiple_of(i * 256, 256), 256)
             step[columns, :] = times(transit[...], earlier[:, columns]).T.astype(jnp.bfloat16)
@@ -199,8 +203,16 @@
         near.wait_recv()
         current[...] = incoming[...]
 
-    parts = times(split_rows(current[...]), step[...])
-    produced[...] = jnp.sum(parts, axis=0, keepdims=True) + step_offset[...]
+    @pl.when(in_turn)
+    def _():
+        between = apply_rows(earlier[...], current[...]) + offset_in[...]
+        produced[...] = apply_rows(transit[...], between) + offset[...]
+
+    @pl.when(jnp.logical_or(even, composed))
+    def _():
+        parts = times(split_rows(current[...]), step[...])
+        produced[...] = jnp.sum(parts, axis=0, keepdims=True) + step_offset[...]
+
     sends = jnp.logical_and(odd, me < n - 1)
 
     @pl.when(sends)

time: 56.5 us -> 54.3 us (0.961)
  Pallas kernels: 47.6 us -> 45.5 us
    pallas_call x1, Pallas kernels: 36.2 us -> 34 us  [shards(): pl.pallas_call(functools.partial(chain_kernel, n), out_shape=(jax.ShapeDt...]
where the time goes in v4:
time: 54.3 us; the launch traced here: 54.1 us
  Pallas kernels  45.5 us (84%)
  local copies, waits for them, and re-layouts  6.08 us (11%)
  between operations  2.5 us (5%)
    pallas_call x1, Pallas kernels, shards(): pl.pallas_call(functools.partial(chain_kernel, n), out_shape=(jax.ShapeDt...  34 us
    pallas_call x1, Pallas kernels, shards(): pl.pallas_call(observe_kernel, out_shape=(jax.ShapeDtypeStruct((NE, N), b...  11.4 us
    unnamed x19, local copies, waits for them, and re-layouts  6.08 us

profile of v4, /device:TPU:0, one launch (start us, length us, event | category | flops | bytes accessed | tf_op | source)
XLA Modules:
  0.0 54.1 jit_solution(8474924570863930091)
XLA Ops:
  1.3 0.0 copy-start
  1.3 1.6 %copy-done = bf16[1024,1024]{1,0:T(8,128)(2,1)S(1)} copy-done((bf16[1024,1024]{1,0:T(8,128)(2,1)S(1)}, bf16[1024,1024]{1,0:T(8,128)(2,1)}, u32[]{:S(2)}) %copy-start) | copy-done | bytes 2097176
  2.9 0.0 copy-start.2
  2.9 0.9 %copy-done.2 = bf16[1024,128]{1,0:T(8,128)(2,1)S(1)} copy-done((bf16[1024,128]{1,0:T(8,128)(2,1)S(1)}, bf16[1024,128]{1,0:T(8,128)(2,1)}, u32[]{:S(2)}) %copy-start.2) | copy-done | bytes 262168
  3.8 0.0 copy-start.4
  3.8 0.9 %copy-done.4 = bf16[1,256,256]{2,1,0:T(8,128)(2,1)S(1)} copy-done((bf16[1,256,256]{2,1,0:T(8,128)(2,1)S(1)}, bf16[1,256,256]{2,1,0:T(8,128)(2,1)}, u32[]{:S(2)}) %copy-start.4) | copy-done | bytes 131096
  4.7 0.0 copy-start.6
  4.7 0.7 %copy-done.6 = s32[1,2,2]{2,1,0:T(2,128)S(1)} copy-done((s32[1,2,2]{2,1,0:T(2,128)S(1)}, s32[1,2,2]{2,1,0:T(2,128)}, u32[]{:S(2)}) %copy-start.6) | copy-done | bytes 40
  5.4 0.0 copy-start.7
  5.4 0.7 %copy-done.7 = f32[1,256]{1,0:T(1,128)S(1)} copy-done((f32[1,256]{1,0:T(1,128)S(1)}, f32[1,256]{1,0:T(1,128)}, u32[]{:S(2)}) %copy-start.7) | copy-done | bytes 1048
  6.1 0.0 copy-start.8
  6.1 0.7 %copy-done.8 = f32[1,256]{1,0:T(1,128)S(1)} copy-done((f32[1,256]{1,0:T(1,128)S(1)}, f32[1,256]{1,0:T(1,128)}, u32[]{:S(2)}) %copy-start.8) | copy-done | bytes 1048
  6.8 0.0 copy-start.1
  6.8 0.0 copy-start.3
  6.8 0.0 copy-start.5
  6.8 11.4 %observe.1 = (bf16[128,1024]{1,0:T(8,128)(2,1)S(1)}, f32[1,1024]{1,0:T(1,128)S(1)}, f32[256,1024]{1,0:T(8,128)S(1)}, f32[128,256]{1,0:T(8,128)S(1)}, f32[256,128...) custom-call(s32[1,2,2]{2,1,0:T(2,128)S(1)} %copy-done.6, s32[1]{0:T(128)S(6)} %copy.12.count, ...), custom_call_target="tpu_custom_call" | custom-call | tf_op jit(solution)/shard_map/observe/pallas_call | solution.py:296
  18.2 0.0 copy-done.1
  18.2 0.0 copy-done.3
  18.2 0.0 copy-done.5
  18.2 34.0 %chain.1 = (f32[1,1024]{1,0:T(1,128)S(1)}, f32[1,128]{1,0:T(1,128)S(1)}) custom-call(s32[1]{0:T(128)S(6)} %copy.12.count, bf16[1024,1024]{1,0:T(8,128)(2,1)S(1)} %copy-done.1, bf16[1024,128]{1,0:T(8,128)(2,1)S(1)} %copy-done.3, bf16[128,1024]{1,0:T(8,128)(2,1)S(1)} %get-tuple-element.11.reduced, f32[1,1024]{1,0:T(1,128)S(1)} %get-tuple-element.12.offset, ...), custom_call_target="tpu_custom_call" | custom-call | tf_op jit(solution)/shard_map/chain/pallas_call | solution.py:317
  52.3 0.6 %copy.13 = f32[1,1024]{1,0:T(1,128)} copy(f32[1,1024]{1,0:T(1,128)S(1)} %get-tuple-element.22) | data formatting | bytes 8192
Async XLA Ops:
  1.3 1.6 %copy-start = (bf16[1024,1024]{1,0:T(8,128)(2,1)S(1)}, bf16[1024,1024]{1,0:T(8,128)(2,1)}, u32[]{:S(2)}) copy-start(bf16[1024,1024]{1,0:T(8,128)(2,1)} %trans_hbm.3) | copy-start | bytes 6291460
  2.9 0.9 %copy-start.2 = (bf16[1024,128]{1,0:T(8,128)(2,1)S(1)}, bf16[1024,128]{1,0:T(8,128)(2,1)}, u32[]{:S(2)}) copy-start(bf16[1024,128]{1,0:T(8,128)(2,1)} %ensemble.3) | copy-start | bytes 786436
  3.8 0.9 %copy-start.4 = (bf16[1,256,256]{2,1,0:T(8,128)(2,1)S(1)}, bf16[1,256,256]{2,1,0:T(8,128)(2,1)}, u32[]{:S(2)}) copy-start(bf16[1,256,256]{2,1,0:T(8,128)(2,1)} %hrows.1) | copy-start | bytes 393220
  4.7 0.7 %copy-start.6 = (s32[1,2,2]{2,1,0:T(2,128)S(1)}, s32[1,2,2]{2,1,0:T(2,128)}, u32[]{:S(2)}) copy-start(s32[1,2,2]{2,1,0:T(2,128)} %pattern.1) | copy-start | bytes 52
  5.4 0.7 %copy-start.7 = (f32[1,256]{1,0:T(1,128)S(1)}, f32[1,256]{1,0:T(1,128)}, u32[]{:S(2)}) copy-start(f32[1,256]{1,0:T(1,128)} %yobs.1) | copy-start | bytes 3076
  6.1 0.7 %copy-start.8 = (f32[1,256]{1,0:T(1,128)S(1)}, f32[1,256]{1,0:T(1,128)}, u32[]{:S(2)}) copy-start(f32[1,256]{1,0:T(1,128)} %rvar.1) | copy-start | bytes 3076
  6.8 11.5 %copy-start.1 = (bf16[1024,1024]{1,0:T(8,128)(2,1)S(1)}, bf16[1024,1024]{1,0:T(8,128)(2,1)}, u32[]{:S(2)}) copy-start(bf16[1024,1024]{1,0:T(8,128)(2,1)} %trans_hbm.3) | copy-start | bytes 6291460
  6.8 11.5 %copy-start.3 = (bf16[1024,128]{1,0:T(8,128)(2,1)S(1)}, bf16[1024,128]{1,0:T(8,128)(2,1)}, u32[]{:S(2)}) copy-start(bf16[1024,128]{1,0:T(8,128)(2,1)} %ensemble.3) | copy-start | bytes 786436
  6.8 11.5 %copy-start.5 = (f32[1024]{0:T(1024)S(1)}, f32[1024]{0:T(1024)}, u32[]{:S(2)}) copy-start(f32[1024]{0:T(1024)} %param.15) | copy-start | bytes 12292

commit v5 on v4

--- a/solution.py
+++ b/solution.py
@@ -125,8 +125,9 @@
     me = lax.axis_index("tm")
     odd = lax.rem(me, 2) == 1
     even = lax.rem(me, 2) == 0
-    in_turn = jnp.logical_and(odd, me < 4)
-    composed = jnp.logical_and(odd, me >= 4)
+    sends = jnp.logical_and(odd, me < n - 1)
+    in_turn = jnp.logical_and(sends, me < 4)
+    composed = jnp.logical_and(sends, me >= 4)
     fetch = pltpu.make_async_copy(trans_hbm, trans, trans_sem)
     fetch.start()
     barrier = pltpu.get_barrier_semaphore()
@@ -208,19 +209,15 @@
         between = apply_rows(earlier[...], current[...]) + offset_in[...]
         produced[...] = apply_rows(transit[...], between) + offset[...]
 
-    @pl.when(jnp.logical_or(even, composed))
+    @pl.when(composed)
     def _():
         parts = times(split_rows(current[...]), step[...])
         produced[...] = jnp.sum(parts, axis=0, keepdims=True) + step_offset[...]
 
-    sends = jnp.logical_and(odd, me < n - 1)
-
     @pl.when(sends)
     def _():
         far.start()
         near.start()
-
-    states[...] = produced[...]
 
     @pl.when(odd)
     def _():
@@ -268,6 +265,17 @@
         return carry
 
     lax.fori_loop(1, n, start, 0)
+
+    @pl.when(even)
+    def _():
+        parts = times(split_rows(current[...]), step[...])
+        produced[...] = jnp.sum(parts, axis=0, keepdims=True) + step_offset[...]
+
+    @pl.when(me == n - 1)
+    def _():
+        produced[...] = apply_rows(transit[...], current[...]) + offset[...]
+
+    states[...] = produced[...]
     lax.fori_loop(1, n, finish, 0)
     lax.fori_loop(1, n, sent, 0)
 

time: 54.3 us -> 53.9 us (level)
  no operation moved by 1% of the time
where the time goes in v5:
time: 53.9 us; the launch traced here: 53.6 us
  Pallas kernels  45 us (83%)
  local copies, waits for them, and re-layouts  6.08 us (11%)
  between operations  2.5 us (5%)
    pallas_call x1, Pallas kernels, shards(): pl.pallas_call(functools.partial(chain_kernel, n), out_shape=(jax.ShapeDt...  33.6 us
    pallas_call x1, Pallas kernels, shards(): pl.pallas_call(observe_kernel, out_shape=(jax.ShapeDtypeStruct((NE, N), b...  11.4 us
    unnamed x19, local copies, waits for them, and re-layouts  6.08 us

profile of v5, /device:TPU:0, one launch (start us, length us, event | category | flops | bytes accessed | tf_op | source)
XLA Modules:
  0.0 53.6 jit_solution(11496416109545169913)
XLA Ops:
  1.3 0.0 copy-start
  1.3 1.6 %copy-done = bf16[1024,1024]{1,0:T(8,128)(2,1)S(1)} copy-done((bf16[1024,1024]{1,0:T(8,128)(2,1)S(1)}, bf16[1024,1024]{1,0:T(8,128)(2,1)}, u32[]{:S(2)}) %copy-start) | copy-done | bytes 2097176
  2.9 0.0 copy-start.2
  2.9 0.9 %copy-done.2 = bf16[1024,128]{1,0:T(8,128)(2,1)S(1)} copy-done((bf16[1024,128]{1,0:T(8,128)(2,1)S(1)}, bf16[1024,128]{1,0:T(8,128)(2,1)}, u32[]{:S(2)}) %copy-start.2) | copy-done | bytes 262168
  3.8 0.0 copy-start.4
  3.8 0.9 %copy-done.4 = bf16[1,256,256]{2,1,0:T(8,128)(2,1)S(1)} copy-done((bf16[1,256,256]{2,1,0:T(8,128)(2,1)S(1)}, bf16[1,256,256]{2,1,0:T(8,128)(2,1)}, u32[]{:S(2)}) %copy-start.4) | copy-done | bytes 131096
  4.7 0.0 copy-start.6
  4.7 0.7 %copy-done.6 = s32[1,2,2]{2,1,0:T(2,128)S(1)} copy-done((s32[1,2,2]{2,1,0:T(2,128)S(1)}, s32[1,2,2]{2,1,0:T(2,128)}, u32[]{:S(2)}) %copy-start.6) | copy-done | bytes 40
  5.4 0.0 copy-start.7
  5.4 0.7 %copy-done.7 = f32[1,256]{1,0:T(1,128)S(1)} copy-done((f32[1,256]{1,0:T(1,128)S(1)}, f32[1,256]{1,0:T(1,128)}, u32[]{:S(2)}) %copy-start.7) | copy-done | bytes 1048
  6.1 0.0 copy-start.8
  6.1 0.7 %copy-done.8 = f32[1,256]{1,0:T(1,128)S(1)} copy-done((f32[1,256]{1,0:T(1,128)S(1)}, f32[1,256]{1,0:T(1,128)}, u32[]{:S(2)}) %copy-start.8) | copy-done | bytes 1048
  6.8 0.0 copy-start.1
  6.8 0.0 copy-start.3
  6.8 0.0 copy-start.5
  6.8 11.4 %observe.1 = (bf16[128,1024]{1,0:T(8,128)(2,1)S(1)}, f32[1,1024]{1,0:T(1,128)S(1)}, f32[256,1024]{1,0:T(8,128)S(1)}, f32[128,256]{1,0:T(8,128)S(1)}, f32[256,128...) custom-call(s32[1,2,2]{2,1,0:T(2,128)S(1)} %copy-done.6, s32[1]{0:T(128)S(6)} %copy.12.count, ...), custom_call_target="tpu_custom_call" | custom-call | tf_op jit(solution)/shard_map/observe/pallas_call | solution.py:304
  18.2 0.0 copy-done.1
  18.2 0.0 copy-done.3
  18.2 0.0 copy-done.5
  18.2 33.6 %chain.1 = (f32[1,1024]{1,0:T(1,128)S(1)}, f32[1,128]{1,0:T(1,128)S(1)}) custom-call(s32[1]{0:T(128)S(6)} %copy.12.count, bf16[1024,1024]{1,0:T(8,128)(2,1)S(1)} %copy-done.1, bf16[1024,128]{1,0:T(8,128)(2,1)S(1)} %copy-done.3, bf16[128,1024]{1,0:T(8,128)(2,1)S(1)} %get-tuple-element.11.reduced, f32[1,1024]{1,0:T(1,128)S(1)} %get-tuple-element.12.offset, ...), custom_call_target="tpu_custom_call" | custom-call | tf_op jit(solution)/shard_map/chain/pallas_call | solution.py:325
  51.8 0.6 %copy.13 = f32[1,1024]{1,0:T(1,128)} copy(f32[1,1024]{1,0:T(1,128)S(1)} %get-tuple-element.22) | data formatting | bytes 8192
Async XLA Ops:
  1.3 1.6 %copy-start = (bf16[1024,1024]{1,0:T(8,128)(2,1)S(1)}, bf16[1024,1024]{1,0:T(8,128)(2,1)}, u32[]{:S(2)}) copy-start(bf16[1024,1024]{1,0:T(8,128)(2,1)} %trans_hbm.3) | copy-start | bytes 6291460
  2.9 0.9 %copy-start.2 = (bf16[1024,128]{1,0:T(8,128)(2,1)S(1)}, bf16[1024,128]{1,0:T(8,128)(2,1)}, u32[]{:S(2)}) copy-start(bf16[1024,128]{1,0:T(8,128)(2,1)} %ensemble.3) | copy-start | bytes 786436
  3.8 0.9 %copy-start.4 = (bf16[1,256,256]{2,1,0:T(8,128)(2,1)S(1)}, bf16[1,256,256]{2,1,0:T(8,128)(2,1)}, u32[]{:S(2)}) copy-start(bf16[1,256,256]{2,1,0:T(8,128)(2,1)} %hrows.1) | copy-start | bytes 393220
  4.7 0.7 %copy-start.6 = (s32[1,2,2]{2,1,0:T(2,128)S(1)}, s32[1,2,2]{2,1,0:T(2,128)}, u32[]{:S(2)}) copy-start(s32[1,2,2]{2,1,0:T(2,128)} %pattern.1) | copy-start | bytes 52
  5.4 0.7 %copy-start.7 = (f32[1,256]{1,0:T(1,128)S(1)}, f32[1,256]{1,0:T(1,128)}, u32[]{:S(2)}) copy-start(f32[1,256]{1,0:T(1,128)} %yobs.1) | copy-start | bytes 3076
  6.1 0.7 %copy-start.8 = (f32[1,256]{1,0:T(1,128)S(1)}, f32[1,256]{1,0:T(1,128)}, u32[]{:S(2)}) copy-start(f32[1,256]{1,0:T(1,128)} %rvar.1) | copy-start | bytes 3076
  6.8 11.5 %copy-start.1 = (bf16[1024,1024]{1,0:T(8,128)(2,1)S(1)}, bf16[1024,1024]{1,0:T(8,128)(2,1)}, u32[]{:S(2)}) copy-start(bf16[1024,1024]{1,0:T(8,128)(2,1)} %trans_hbm.3) | copy-start | bytes 6291460
  6.8 11.5 %copy-start.3 = (bf16[1024,128]{1,0:T(8,128)(2,1)S(1)}, bf16[1024,128]{1,0:T(8,128)(2,1)}, u32[]{:S(2)}) copy-start(bf16[1024,128]{1,0:T(8,128)(2,1)} %ensemble.3) | copy-start | bytes 786436
  6.8 11.5 %copy-start.5 = (f32[1024]{0:T(1024)S(1)}, f32[1024]{0:T(1024)}, u32[]{:S(2)}) copy-start(f32[1024]{0:T(1024)} %param.15) | copy-start | bytes 12292
